TPU v7x, 32 devices: a whole 2x2x4 slice. The times are simulated.
32 devices in a mesh: batch: 16 (over z, y, x), seq: 2 (over core).
Axes of the slice: x: 2, y: 2, z: 4, core: 2. Of those that a mesh axis runs over, the one named last changes fastest.
Arguments:
- tokens: bfloat16 [16, 1024, 1024], P('batch', 'seq'), may hold values from -6 to 6
- cotangent: bfloat16 [16, 1024, 1024], P('batch', 'seq'), may hold values from -6 to 6
- w_in: float32 [1024, 3072], P(('batch', 'seq')), may hold values from -0.1875 to 0.1875
- first_in: float32 [1024, 3072], P(('batch', 'seq')), may hold values from -96 to 96
- second_in: float32 [1024, 3072], P(('batch', 'seq')), may hold values from 1146.88 to 7045.12
- conv_taps: float32 [1024, 3], P(('batch', 'seq')), may hold values from -3.5 to 3.5
- first_conv: float32 [1024, 3], P(('batch', 'seq')), may hold values from -96 to 96
- second_conv: float32 [1024, 3], P(('batch', 'seq')), may hold values from 1146.88 to 7045.12
- w_out: float32 [1024, 1024], P(('batch', 'seq')), may hold values from -0.1875 to 0.1875
- first_out: float32 [1024, 1024], P(('batch', 'seq')), may hold values from -96 to 96
- second_out: float32 [1024, 1024], P(('batch', 'seq')), may hold values from 1146.88 to 7045.12
- w_mlp: float32 [1024, 9216], P(('batch', 'seq')), may hold values from -0.1875 to 0.1875
- first_mlp: float32 [1024, 9216], P(('batch', 'seq')), may hold values from -24 to 24
- second_mlp: float32 [1024, 9216], P(('batch', 'seq')), may hold values from 73.728 to 442.368
- w_down: float32 [4608, 1024], P(('batch', 'seq')), may hold values from -0.09375 to 0.09375
- first_down: float32 [4608, 1024], P(('batch', 'seq')), may hold values from -48 to 48
- second_down: float32 [4608, 1024], P(('batch', 'seq')), may hold values from 294.912 to 1802.24
- norm_gains: float32 [1024, 2], P(('batch', 'seq')), may hold values from 0.5 to 1.5
- first_gains: float32 [1024, 2], P(('batch', 'seq')), may hold values from -160 to 160
- second_gains: float32 [1024, 2], P(('batch', 'seq')), may hold values from 3276.8 to 19660.8
Outputs:
- output: bfloat16 [16, 1024, 1024], P('batch', 'seq')
- grad_tokens: bfloat16 [16, 1024, 1024], P('batch', 'seq')
- first_in_next: float32 [1024, 3072], P(('batch', 'seq'))
- second_in_next: float32 [1024, 3072], P(('batch', 'seq'))
- w_in_next: float32 [1024, 3072], P(('batch', 'seq'))
- first_conv_next: float32 [1024, 3], P(('batch', 'seq'))
- second_conv_next: float32 [1024, 3], P(('batch', 'seq'))
- conv_taps_next: float32 [1024, 3], P(('batch', 'seq'))
- first_out_next: float32 [1024, 1024], P(('batch', 'seq'))
- second_out_next: float32 [1024, 1024], P(('batch', 'seq'))
- w_out_next: float32 [1024, 1024], P(('batch', 'seq'))
- first_mlp_next: float32 [1024, 9216], P(('batch', 'seq'))
- second_mlp_next: float32 [1024, 9216], P(('batch', 'seq'))
- w_mlp_next: float32 [1024, 9216], P(('batch', 'seq'))
- first_down_next: float32 [4608, 1024], P(('batch', 'seq'))
- second_down_next: float32 [4608, 1024], P(('batch', 'seq'))
- w_down_next: float32 [4608, 1024], P(('batch', 'seq'))
- first_gains_next: float32 [1024, 2], P(('batch', 'seq'))
- second_gains_next: float32 [1024, 2], P(('batch', 'seq'))
- norm_gains_next: float32 [1024, 2], P(('batch', 'seq'))
All inputs are finite; a program needn't handle non-finite values.
Results may differ from a plain program's by a relative error of at most 0.012.
The roundings to bfloat16 on the way count: a program that leaves them out, or rounds other values in their place, can miss the bound.
Values may be sent and summed in bfloat16 or wider, within the bound.
A program may use at most 256 MiB of HBM per device.

v0:
```python
import jax
import jax.numpy as jnp
from jax import lax
from jax.sharding import PartitionSpec as P

D = 1024
FF = 4608
STEP = 10


EPS = 1e-05
BETA_ONE = 0.9
BETA_TWO = 0.95
ADAM_EPS = 1e-08
DECAY = 0.1


def from_behind(block, axis, distance):
    devices = range(lax.axis_size(axis))
    route = [(i - distance, i) for i in devices if i - distance in devices]
    return lax.ppermute(block, axis, route)


def rms_scale(values):
    return lax.rsqrt(jnp.mean(values * values, axis=-1, keepdims=True) + EPS)


def norm_back(values, inv_scale, gain_row, grad_normed):
    weighted = grad_normed * gain_row
    gain_grad = jnp.sum(grad_normed * values * inv_scale, axis=(0, 1))
    projection = jnp.mean(weighted * values, axis=-1, keepdims=True)
    grad_values = inv_scale * weighted - values * (inv_scale * inv_scale * inv_scale) * projection
    return (grad_values, gain_grad)


def adamw(weight, gradient, first_moment, second_moment, learn_rate):
    new_first = BETA_ONE * first_moment + (1.0 - BETA_ONE) * gradient
    new_second = BETA_TWO * second_moment + (1.0 - BETA_TWO) * gradient * gradient
    first_hat = new_first / (1.0 - BETA_ONE**STEP)
    second_hat = new_second / (1.0 - BETA_TWO**STEP)
    new_weight = weight - learn_rate * (
        first_hat / (jnp.sqrt(second_hat) + ADAM_EPS) + DECAY * weight
    )
    return (new_first, new_second, new_weight)


def shards(
    tokens,
    cotangent,
    w_in,
    first_in,
    second_in,
    conv_taps,
    first_conv,
    second_conv,
    w_out,
    first_out,
    second_out,
    w_mlp,
    first_mlp,
    second_mlp,
    w_down,
    first_down,
    second_down,
    norm_gains,
    first_gains,
    second_gains,
):
    half_type = jnp.bfloat16
    gathered = (
        lax.all_gather(w_in.astype(half_type), ("batch", "seq"), axis=0, tiled=True),
        lax.all_gather(conv_taps.astype(half_type), ("batch", "seq"), axis=0, tiled=True),
        lax.all_gather(w_out.astype(half_type), ("batch", "seq"), axis=0, tiled=True),
        lax.all_gather(w_mlp.astype(half_type), ("batch", "seq"), axis=0, tiled=True),
        lax.all_gather(w_down.astype(half_type), ("batch", "seq"), axis=0, tiled=True),
        lax.all_gather(norm_gains.astype(half_type), ("batch", "seq"), axis=0, tiled=True),
    )
    in_low, conv_low, out_low, mlp_low, down_low, gain_low = gathered
    tap_values = conv_low.astype(jnp.float32)
    gain_one = gain_low[:, 0].astype(jnp.float32)
    gain_two = gain_low[:, 1].astype(jnp.float32)
    inputs = tokens.astype(jnp.float32)
    scale_one = rms_scale(inputs)
    normed = (inputs * scale_one * gain_one).astype(half_type)
    projected = jnp.einsum("spd,de->spe", normed, in_low, preferred_element_type=jnp.float32)
    b_gate = projected[..., :D]
    c_gate = projected[..., D : 2 * D]
    values = projected[..., 2 * D :]
    gated_rows = (b_gate * values).astype(half_type)
    length = gated_rows.shape[1]
    earlier = from_behind(gated_rows[:, length - 2 :], "seq", 1)
    padded = jnp.concatenate([earlier, gated_rows], axis=1).astype(jnp.float32)
    conv_out = (
        padded[:, :length] * tap_values[:, 0]
        + padded[:, 1 : length + 1] * tap_values[:, 1]
        + padded[:, 2:] * tap_values[:, 2]
    )
    mixed_rows = (c_gate * conv_out).astype(half_type)
    branch = jnp.einsum("spd,de->spe", mixed_rows, out_low, preferred_element_type=jnp.float32)
    middle = inputs + branch
    scale_two = rms_scale(middle)
    normed_two = (middle * scale_two * gain_two).astype(half_type)
    gate_up = jnp.einsum("spd,de->spe", normed_two, mlp_low, preferred_element_type=jnp.float32)
    gate_part = gate_up[..., :FF]
    upward = gate_up[..., FF:]
    hidden = (jax.nn.silu(gate_part) * upward).astype(half_type)
    output = (
        middle + jnp.einsum("spf,fd->spd", hidden, down_low, preferred_element_type=jnp.float32)
    ).astype(half_type)
    regathered = (
        lax.all_gather(w_in.astype(half_type), ("batch", "seq"), axis=0, tiled=True),
        lax.all_gather(conv_taps.astype(half_type), ("batch", "seq"), axis=0, tiled=True),
        lax.all_gather(w_out.astype(half_type), ("batch", "seq"), axis=0, tiled=True),
        lax.all_gather(w_mlp.astype(half_type), ("batch", "seq"), axis=0, tiled=True),
        lax.all_gather(w_down.astype(half_type), ("batch", "seq"), axis=0, tiled=True),
        lax.all_gather(norm_gains.astype(half_type), ("batch", "seq"), axis=0, tiled=True),
    )
    in_low, conv_low, out_low, mlp_low, down_low, gain_low = regathered
    tap_values = conv_low.astype(jnp.float32)
    gain_one = gain_low[:, 0].astype(jnp.float32)
    gain_two = gain_low[:, 1].astype(jnp.float32)
    grad_hidden = jnp.einsum("spd,fd->spf", cotangent, down_low, preferred_element_type=jnp.float32)
    sigmoid_gate = jax.nn.sigmoid(gate_part)
    grad_gate = grad_hidden * upward * (sigmoid_gate * (1.0 + gate_part * (1.0 - sigmoid_gate)))
    grad_upward = grad_hidden * (gate_part * sigmoid_gate)
    grad_gate_up = jnp.concatenate([grad_gate, grad_upward], axis=-1).astype(half_type)
    grad_normed_two = jnp.einsum(
        "spe,de->spd", grad_gate_up, mlp_low, preferred_element_type=jnp.float32
    )
    grad_middle, gain_grad_two = norm_back(middle, scale_two, gain_two, grad_normed_two)
    grad_middle = cotangent.astype(jnp.float32) + grad_middle
    grad_branch = grad_middle.astype(half_type)
    grad_mixed = jnp.einsum("spe,de->spd", grad_branch, out_low, preferred_element_type=jnp.float32)
    grad_cgate = grad_mixed * conv_out
    grad_conv = (grad_mixed * c_gate).astype(half_type)
    later = from_behind(grad_conv[:, :2], "seq", -1)
    extended = jnp.concatenate([grad_conv, later], axis=1).astype(jnp.float32)
    grad_taps = jnp.stack(
        [
            jnp.sum(extended[:, :length] * padded[:, offset : offset + length], axis=(0, 1))
            for offset in range(3)
        ],
        axis=-1,
    )
    grad_gated = (
        extended[:, :length] * tap_values[:, 2]
        + extended[:, 1 : length + 1] * tap_values[:, 1]
        + extended[:, 2:] * tap_values[:, 0]
    )
    grad_proj = jnp.concatenate(
        [grad_gated * values, grad_cgate, grad_gated * b_gate], axis=-1
    ).astype(half_type)
    grad_normed = jnp.einsum("spe,de->spd", grad_proj, in_low, preferred_element_type=jnp.float32)
    grad_inputs, gain_grad_one = norm_back(inputs, scale_one, gain_one, grad_normed)
    grad_tokens = (grad_middle + grad_inputs).astype(half_type)
    small_grads = jnp.concatenate(
        [grad_taps, jnp.stack([gain_grad_one, gain_grad_two], axis=-1)], axis=-1
    )
    part_in = jnp.einsum("spd,spe->de", normed, grad_proj, preferred_element_type=jnp.float32)
    part_out = jnp.einsum(
        "spd,spe->de", mixed_rows, grad_branch, preferred_element_type=jnp.float32
    )
    part_mlp = jnp.einsum(
        "spd,spe->de", normed_two, grad_gate_up, preferred_element_type=jnp.float32
    )
    reduced_wide = lax.psum_scatter(
        jnp.concatenate([part_in, part_out, part_mlp, small_grads], axis=1),
        ("batch", "seq"),
        scatter_dimension=0,
        tiled=True,
    )
    grad_down = lax.psum_scatter(
        jnp.einsum("spf,spd->fd", hidden, cotangent, preferred_element_type=jnp.float32),
        ("batch", "seq"),
        scatter_dimension=0,
        tiled=True,
    )
    grad_inw = reduced_wide[:, : 3 * D]
    grad_outw = reduced_wide[:, 3 * D : 4 * D]
    grad_mlp = reduced_wide[:, 4 * D : 4 * D + 2 * FF]
    grad_tapw = reduced_wide[:, 4 * D + 2 * FF : 4 * D + 2 * FF + 3]
    grad_gains = reduced_wide[:, 4 * D + 2 * FF + 3 :]
    rate_wide = 2.0 / D**0.5
    rate_down = 2.0 / FF**0.5
    in_new = adamw(w_in, grad_inw, first_in, second_in, rate_wide)
    conv_new = adamw(conv_taps, grad_tapw, first_conv, second_conv, 1.0)
    out_new = adamw(w_out, grad_outw, first_out, second_out, rate_wide)
    mlp_new = adamw(w_mlp, grad_mlp, first_mlp, second_mlp, rate_wide)
    down_new = adamw(w_down, grad_down, first_down, second_down, rate_down)
    gains_new = adamw(norm_gains, grad_gains, first_gains, second_gains, 0.6)
    return (
        output,
        grad_tokens,
        in_new[0],
        in_new[1],
        in_new[2],
        conv_new[0],
        conv_new[1],
        conv_new[2],
        out_new[0],
        out_new[1],
        out_new[2],
        mlp_new[0],
        mlp_new[1],
        mlp_new[2],
        down_new[0],
        down_new[1],
        down_new[2],
        gains_new[0],
        gains_new[1],
        gains_new[2],
    )


def solution(mesh):
    placed = (
        P("batch", "seq", None),
        P("batch", "seq", None),
        P(("batch", "seq"), None),
        P(("batch", "seq"), None),
        P(("batch", "seq"), None),
        P(("batch", "seq"), None),
        P(("batch", "seq"), None),
        P(("batch", "seq"), None),
        P(("batch", "seq"), None),
        P(("batch", "seq"), None),
        P(("batch", "seq"), None),
        P(("batch", "seq"), None),
        P(("batch", "seq"), None),
        P(("batch", "seq"), None),
        P(("batch", "seq"), None),
        P(("batch", "seq"), None),
        P(("batch", "seq"), None),
        P(("batch", "seq"), None),
        P(("batch", "seq"), None),
        P(("batch", "seq"), None),
    )
    return jax.shard_map(
        shards,
        mesh=mesh,
        in_specs=placed,
        out_specs=(
            P("batch", "seq", None),
            P("batch", "seq", None),
            P(("batch", "seq"), None),
            P(("batch", "seq"), None),
            P(("batch", "seq"), None),
            P(("batch", "seq"), None),
            P(("batch", "seq"), None),
            P(("batch", "seq"), None),
            P(("batch", "seq"), None),
            P(("batch", "seq"), None),
            P(("batch", "seq"), None),
            P(("batch", "seq"), None),
            P(("batch", "seq"), None),
            P(("batch", "seq"), None),
            P(("batch", "seq"), None),
            P(("batch", "seq"), None),
            P(("batch", "seq"), None),
            P(("batch", "seq"), None),
            P(("batch", "seq"), None),
            P(("batch", "seq"), None),
        ),
        check_vma=False,
    )
```

profile of v0, /device:TPU:0, one launch (start us, length us, event | category | flops | bytes accessed | tf_op | source)
XLA Modules:
  0.0 1111.4 jit_solution(2602739806579901614)
XLA Ops:
  13.9 43.0 %all-gather = bf16[32,32,2]{1,2,0:T(2,128)(2,1)S(1)} all-gather(bf16[1,32,2]{1,2,0:T(2,128)(2,1)S(1)} %convert_bitcast_fusion.1), channel_id=1, replica_groups=mesh['batch'=16,'seq'=2] {'batch','seq'}, dimensions={0}, use_global_device_ids=true | all-gather | bytes 4224 | tf_op jit(solution)/shard_map/all_gather | solution.py:76
  57.0 36.8 %all-gather.1 = bf16[32,32,3]{1,2,0:T(4,128)(2,1)S(1)} all-gather(bf16[1,32,3]{1,2,0:T(4,128)(2,1)S(1)} %convert_bitcast_fusion), channel_id=1, replica_groups=mesh['batch'=16,'seq'=2] {'batch','seq'}, dimensions={0}, use_global_device_ids=true | all-gather | bytes 6336 | tf_op jit(solution)/shard_map/all_gather | solution.py:72
  94.8 5.7 convolution_bitcast_fusion.1
  106.6 35.5 %all-gather.9.cloned.1.call-done = bf16[1024,1024]{1,0:T(8,128)(2,1)} async-done(((bf16[32,1024]{1,0:T(8,128)(2,1)}), bf16[1024,1024]{1,0:T(8,128)(2,1)}) %all-gather.9.cloned.1.call-update) | async-done | bytes 2097168 | tf_op jit(solution)/shard_map/all_gather | solution.py:73
  142.2 4.5 multiply_reduce_fusion.3
  146.7 122.5 %all-gather.11.cloned.1.call-done = bf16[1024,9216]{1,0:T(8,128)(2,1)} async-done(((bf16[32,9216]{1,0:T(8,128)(2,1)}), bf16[1024,9216]{1,0:T(8,128)(2,1)}) %all-gather.11.cloned.1.call-update) | async-done | bytes 18874384 | tf_op jit(solution)/shard_map/all_gather | solution.py:74
  269.2 18.1 %convolution_bitcast_fusion = f32[1,512,9216]{2,1,0:T(8,128)} fusion(bf16[1024,9216]{1,0:T(8,128)(2,1)} %all-gather.11.cloned.1.call-done, f32[1,512,1024]{2,1,0:T(8,128)} %get-tuple-element.166, f32[1024]{0:T(1024)S(1)} %bitcast.117, f32[512]{0:T(512)S(1)} %get-tuple-element.164), kind=kOutput, calls=%fused_computation | convolution fusion | flops 9665249280 | bytes 39852032 | tf_op jit(solution)/shard_map/spd,de->spe/dot_general | solution.py:103
  287.3 65.4 %all-gather.13.cloned.1.call-done = bf16[4608,1024]{1,0:T(8,128)(2,1)} async-done(((bf16[144,1024]{1,0:T(8,128)(2,1)}), bf16[4608,1024]{1,0:T(8,128)(2,1)}) %all-gather.13.cloned.1.call-update) | async-done | bytes 9437200 | tf_op jit(solution)/shard_map/all_gather | solution.py:75
  352.8 18.0 %fusion.9 = (bf16[512,4608]{1,0:T(8,128)(2,1)}, bf16[512,4608]{1,0:T(8,128)(2,1)}, bf16[512,4608]{1,0:T(8,128)(2,1)}) fusion(f32[1,512,9216]{2,1,0:T(8,128)} %convolution_bitcast_fusion, bf16[4608,1024]{1,0:T(8,128)(2,1)} %all-gather.13.cloned.1.call-done, bf16[1,512,1024]{2,1,0:T(8,128)(2,1)} %param.21), kind=kOutput, calls=%fused_computation.25 | convolution fusion | flops 4867227648 | bytes 43515904 | tf_op jit(solution)/shard_map/spd,fd->spf/dot_general | solution.py:122
  370.8 11.0 fusion.42
  382.1 18.8 %fusion.23 = (f32[1024]{0:T(1024)S(1)}, f32[512]{0:T(512)S(1)}, f32[512,1024]{1,0:T(8,128)S(1)}) fusion(f32[1,512,1024]{2,1,0:T(8,128)} %get-tuple-element.166, f32[512]{0:T(512)S(1)} %get-tuple-element.164, f32[1024]{0:T(1024)S(1)} %bitcast.118, bf16[1024,9216]{1,0:T(8,128)(2,1)} %all-gather.11.cloned.1.call-done, ...), kind=kOutput, calls=%fused_computation.44 | convolution fusion | flops 9685694464 | bytes 32518144 | tf_op jit(solution)/shard_map/spe,de->spd/dot_general | solution.py:127
  410.3 23.0 %fusion.4 = f32[1024,9216]{1,0:T(8,128)} fusion(bf16[512,4608]{1,0:T(8,128)(2,1)} %get-tuple-element.150, bf16[512,4608]{1,0:T(8,128)(2,1)} %get-tuple-element.149, f32[1,512,1024]{2,1,0:T(8,128)S(1)} %copy-done.4, f32[1024]{0:T(1024)S(1)} %bitcast.120, f32[512]{0:T(512)S(1)} %get-tuple-element.164), kind=kOutput, calls=%fused_computation.11 | convolution fusion | flops 9684123648 | bytes 49289216 | tf_op jit(solution)/shard_map/spd,spe->de/dot_general | solution.py:163
  439.1 4.2 multiply_reduce_fusion
  449.2 7.8 fusion.19
  458.1 9.4 fusion.30
  467.5 62.9 %concatenate.60 = f32[1024,13317]{1,0:T(8,128)} concatenate(f32[1024,3072]{1,0:T(8,128)} %fusion.30, f32[1024,1024]{1,0:T(8,128)} %fusion.38, f32[1024,9216]{1,0:T(8,128)} %fusion.4, f32[1024,1]{1,0:T(8,128)} %copy.155, f32[1024,1]{1,0:T(8,128)} %copy.156, f32[1024,1]{1,0:T(8,128)} %copy.157, f32[1024,1]{1,0:T(8,128)} %copy.158, f32[1024,1]{1,0:T(8,128)} %copy.159), dimensions={1} | concatenate | bytes 109092864 | tf_op jit(solution)/shard_map/concatenate | solution.py:167
  545.2 4.0 copy.168
  549.2 10.2 fusion.28
  561.1 26.2 %reduce-scatter.5.cloned.1.call-done = f32[144,1024]{1,0:T(8,128)} async-done(((f32[4608,1024]{1,0:T(8,128)}), f32[144,1024]{1,0:T(8,128)}) %reduce-scatter.5.cloned.1.call-update) | async-done | bytes 589840 | tf_op jit(solution)/shard_map/reduce_scatter | solution.py:172
  590.2 464.7 %reduce-scatter.7.cloned.1.call-done = f32[32,13317]{1,0:T(8,128)} async-done(((f32[1024,13317]{1,0:T(8,128)}), f32[32,13317]{1,0:T(8,128)}) %reduce-scatter.7.cloned.1.call-update) | async-done | bytes 1704592
  1057.6 4.8 multiply_subtract_fusion.1
  1078.4 12.9 %multiply_subtract_fusion = (f32[32,9216]{0,1:T(8,128)}, f32[32,9216]{0,1:T(8,128)}, f32[32,9216]{0,1:T(8,128)}) fusion(f32[32,9216]{0,1:T(8,128)} %copy.171, f32[32,9216]{0,1:T(8,128)} %copy.187, f32[32,9216]{0,1:T(8,128)} %copy.169, f32[32,9216]{0,1:T(8,128)} %copy.168), kind=kLoop, calls=%fused_computation.17 | loop fusion | flops 4423680 | bytes 8257536 | tf_op jit(solution)/shard_map/sub | solution.py:41
  1091.3 3.8 copy.178
  1099.1 4.0 copy.180
  (165 shorter events, 79.0 us)
Async XLA Ops:
  7.2 5.8 copy-start.16
  7.2 87.6 %all-gather.7.cloned.1.call-start = ((), (), s32[]{:S(2)}) async-start(), calls=%async_computation.2 | async-start | bytes 6488064 | tf_op jit(solution)/shard_map/all_gather | solution.py:71
  9.0 48.0 %copy-start.32 = (f32[32,3]{0,1:T(4,128)S(1)}, f32[32,3]{0,1:T(4,128)}, u32[]{:S(2)}) copy-start(f32[32,3]{0,1:T(4,128)} %param.25) | copy-start | bytes 1156
  9.0 84.9 %copy-start.3 = (bf16[1,512,1024]{2,1,0:T(8,128)(2,1)S(1)}, bf16[1,512,1024]{2,1,0:T(8,128)(2,1)}, u32[]{:S(2)}) copy-start(bf16[1,512,1024]{2,1,0:T(8,128)(2,1)} %param.20) | copy-start | bytes 3145732
  9.0 133.1 %all-gather.9.cloned.1.call-start = ((), (), s32[]{:S(2)}) async-start(), calls=%async_computation.3 | async-start | bytes 2162688 | tf_op jit(solution)/shard_map/all_gather | solution.py:73
  10.7 258.5 %all-gather.11.cloned.1.call-start = ((), (), s32[]{:S(2)}) async-start(), calls=%async_computation.4 | async-start | bytes 19464192 | tf_op jit(solution)/shard_map/all_gather | solution.py:74
  12.9 339.8 %all-gather.13.cloned.1.call-start = ((), (), s32[]{:S(2)}) async-start(), calls=%async_computation.5 | async-start | bytes 9732096 | tf_op jit(solution)/shard_map/all_gather | solution.py:75
  13.8 573.5 %reduce-scatter.5.cloned.1.call-start = ((), (), s32[]{:S(2)}) async-start(), calls=%async_computation.6 | async-start | bytes 19464192 | tf_op jit(solution)/shard_map/reduce_scatter | solution.py:172
  100.9 3.0 collective-permute-start
  381.8 673.1 %reduce-scatter.7.cloned.1.call-start = ((), (), s32[]{:S(2)}) async-start(), calls=%async_computation.7 | async-start | bytes 56770560
  382.1 18.9 %copy-start.4 = (f32[1,512,1024]{2,1,0:T(8,128)S(1)}, f32[1,512,1024]{2,1,0:T(8,128)}, u32[]{:S(2)}) copy-start(f32[1,512,1024]{2,1,0:T(8,128)} %get-tuple-element.166) | copy-start | bytes 6291460
  382.1 18.9 %copy-start.24 = (bf16[1,512,1024]{2,1,0:T(8,128)(2,1)S(1)}, bf16[1,512,1024]{2,1,0:T(8,128)(2,1)}, u32[]{:S(2)}) copy-start(bf16[1,512,1024]{2,1,0:T(8,128)(2,1)} %param.21) | copy-start | bytes 3145732
  402.7 30.6 %copy-start.1 = (f32[1,512,1024]{2,1,0:T(8,128)}, f32[1,512,1024]{2,1,0:T(8,128)S(1)}, u32[]{:S(2)}) copy-start(f32[1,512,1024]{2,1,0:T(8,128)S(1)} %fusion.27) | copy-start | bytes 6291460
  408.8 24.5 %copy-start.13 = (bf16[1,512,1024]{2,1,0:T(8,128)(2,1)}, bf16[1,512,1024]{2,1,0:T(8,128)(2,1)S(1)}, u32[]{:S(2)}) copy-start(bf16[1,512,1024]{2,1,0:T(8,128)(2,1)S(1)} %get-tuple-element.155) | copy-start | bytes 3145732
  408.8 24.5 %copy-start.7 = (bf16[512,1024]{1,0:T(8,128)(2,1)S(1)}, bf16[512,1024]{1,0:T(8,128)(2,1)}, u32[]{:S(2)}) copy-start(bf16[512,1024]{1,0:T(8,128)(2,1)} %get-tuple-element.147) | copy-start | bytes 3145732
  408.9 28.8 %collective-permute-start.1 = (bf16[1,2,1024]{2,1,0:T(2,128)(2,1)S(1)}, bf16[1,2,1024]{2,1,0:T(2,128)(2,1)S(1)}, u32[]{:S(2)}, u32[]{:S(2)}) collective-permute-start(bf16[1,2,1024]{2,1,0:T(2,128)(2,1)S(1)} %slice.117), channel_id=1, source_target_pairs={{1,0},{3,2},{5,4},{7,6},{9,8},{11,10},{13,12},{15,14},{17,16},{19,... | collective-permute-start | bytes 12296 | tf_op jit(solution)/shard_map/ppermute | solution.py:21
  549.2 10.3 copy-start.2
  549.2 10.3 copy-start.18
  549.2 10.3 copy-start.31
  559.5 27.8 %copy-start.17 = (f32[144,1024]{1,0:T(8,128)S(1)}, f32[144,1024]{1,0:T(8,128)}, u32[]{:S(2)}) copy-start(f32[144,1024]{1,0:T(8,128)} %param.34) | copy-start | bytes 1769476
  559.5 27.8 %copy-start.25 = (f32[144,1024]{1,0:T(8,128)S(1)}, f32[144,1024]{1,0:T(8,128)}, u32[]{:S(2)}) copy-start(f32[144,1024]{1,0:T(8,128)} %param.36) | copy-start | bytes 1769476
  587.3 470.2 %copy-start.9 = (f32[32,3072]{0,1:T(8,128)S(1)}, f32[32,3072]{0,1:T(8,128)}, u32[]{:S(2)}) copy-start(f32[32,3072]{0,1:T(8,128)} %copy.161) | copy-start | bytes 1179652
  590.2 467.4 %copy-start.8 = (f32[32,3072]{0,1:T(8,128)S(1)}, f32[32,3072]{0,1:T(8,128)}, u32[]{:S(2)}) copy-start(f32[32,3072]{0,1:T(8,128)} %copy.163) | copy-start | bytes 1179652
  1062.4 5.5 copy-start.10
  (28 other events, 100.5 us)
Sparse Core Ops, SparseCore 0:
  11.5 72.2 all-gather.6
  87.2 54.8 all-gather.8
  145.6 123.5 all-gather.10
  272.5 80.2 all-gather.12
  381.9 205.3 reduce-scatter.4
  593.6 461.2 reduce-scatter.6
where the time goes:
time: 1120 us; the launch traced here: 1110 us
  waiting for transfers between devices  715 us (64%)
  matrix products  131 us (12%)
  local copies, waits for them, and re-layouts  119 us (11%)
  blocking collectives  79.8 us (7%)
  other arithmetic  47.4 us (4%)
  between operations  14.8 us (1%)
    unnamed x7, waiting for transfers between devices  465 us
    all_gather x1, waiting for transfers between devices, shards(): lax.all_gather(w_mlp.astype(half_type), ('batch', 'seq'), axis=0, tiled=T...  123 us
    all_gather x1, waiting for transfers between devices, shards(): lax.all_gather(w_down.astype(half_type), ('batch', 'seq'), axis=0, tiled=...  65.4 us
    concatenate x1, local copies, waits for them, and re-layouts, shards(): jnp.concatenate([part_in, part_out, part_mlp, small_grads], axis=1)  62.9 us
    unnamed x106, local copies, waits for them, and re-layouts  49.4 us
    all_gather x1, blocking collectives, shards(): lax.all_gather(norm_gains.astype(half_type), ('batch', 'seq'), axis=0, ti...  43 us
    all_gather x1, blocking collectives, shards(): lax.all_gather(conv_taps.astype(half_type), ('batch', 'seq'), axis=0, til...  36.8 us
    all_gather x1, waiting for transfers between devices, shards(): lax.all_gather(w_out.astype(half_type), ('batch', 'seq'), axis=0, tiled=T...  35.5 us
  transfers between devices with their start and end apart: 8, of which 6 were waited for; matrix products, arithmetic and copies ran while one was open for 19% of the time, Pallas kernels for 0%

commit v1 on v0

--- a/solution.py
+++ b/solution.py
@@ -6,6 +6,7 @@
 D = 1024
 FF = 4608
 STEP = 10
+SMALL = 128
 
 
 EPS = 1e-05
@@ -67,15 +68,26 @@
     second_gains,
 ):
     half_type = jnp.bfloat16
-    gathered = (
-        lax.all_gather(w_in.astype(half_type), ("batch", "seq"), axis=0, tiled=True),
-        lax.all_gather(conv_taps.astype(half_type), ("batch", "seq"), axis=0, tiled=True),
-        lax.all_gather(w_out.astype(half_type), ("batch", "seq"), axis=0, tiled=True),
-        lax.all_gather(w_mlp.astype(half_type), ("batch", "seq"), axis=0, tiled=True),
-        lax.all_gather(w_down.astype(half_type), ("batch", "seq"), axis=0, tiled=True),
-        lax.all_gather(norm_gains.astype(half_type), ("batch", "seq"), axis=0, tiled=True),
-    )
-    in_low, conv_low, out_low, mlp_low, down_low, gain_low = gathered
+    rows = w_in.shape[0]
+    both = ("batch", "seq")
+    spare = jnp.zeros((rows, SMALL - 5), half_type)
+    first_pack = jnp.concatenate(
+        [
+            w_in.astype(half_type),
+            w_out.astype(half_type),
+            conv_taps.astype(half_type),
+            norm_gains.astype(half_type),
+            spare,
+        ],
+        axis=1,
+    )
+    first_low = lax.all_gather(first_pack, both, axis=0, tiled=True)
+    mlp_low = lax.all_gather(w_mlp.astype(half_type), both, axis=0, tiled=True)
+    down_low = lax.all_gather(w_down.astype(half_type), both, axis=0, tiled=True)
+    in_low = first_low[:, : 3 * D]
+    out_low = first_low[:, 3 * D : 4 * D]
+    conv_low = first_low[:, 4 * D : 4 * D + 3]
+    gain_low = first_low[:, 4 * D + 3 : 4 * D + 5]
     tap_values = conv_low.astype(jnp.float32)
     gain_one = gain_low[:, 0].astype(jnp.float32)
     gain_two = gain_low[:, 1].astype(jnp.float32)
@@ -107,18 +119,6 @@
     output = (
         middle + jnp.einsum("spf,fd->spd", hidden, down_low, preferred_element_type=jnp.float32)
     ).astype(half_type)
-    regathered = (
-        lax.all_gather(w_in.astype(half_type), ("batch", "seq"), axis=0, tiled=True),
-        lax.all_gather(conv_taps.astype(half_type), ("batch", "seq"), axis=0, tiled=True),
-        lax.all_gather(w_out.astype(half_type), ("batch", "seq"), axis=0, tiled=True),
-        lax.all_gather(w_mlp.astype(half_type), ("batch", "seq"), axis=0, tiled=True),
-        lax.all_gather(w_down.astype(half_type), ("batch", "seq"), axis=0, tiled=True),
-        lax.all_gather(norm_gains.astype(half_type), ("batch", "seq"), axis=0, tiled=True),
-    )
-    in_low, conv_low, out_low, mlp_low, down_low, gain_low = regathered
-    tap_values = conv_low.astype(jnp.float32)
-    gain_one = gain_low[:, 0].astype(jnp.float32)
-    gain_two = gain_low[:, 1].astype(jnp.float32)
     grad_hidden = jnp.einsum("spd,fd->spf", cotangent, down_low, preferred_element_type=jnp.float32)
     sigmoid_gate = jax.nn.sigmoid(gate_part)
     grad_gate = grad_hidden * upward * (sigmoid_gate * (1.0 + gate_part * (1.0 - sigmoid_gate)))
@@ -153,33 +153,39 @@
     grad_normed = jnp.einsum("spe,de->spd", grad_proj, in_low, preferred_element_type=jnp.float32)
     grad_inputs, gain_grad_one = norm_back(inputs, scale_one, gain_one, grad_normed)
     grad_tokens = (grad_middle + grad_inputs).astype(half_type)
-    small_grads = jnp.concatenate(
-        [grad_taps, jnp.stack([gain_grad_one, gain_grad_two], axis=-1)], axis=-1
-    )
-    part_in = jnp.einsum("spd,spe->de", normed, grad_proj, preferred_element_type=jnp.float32)
+    part_down = jnp.einsum("spf,spd->fd", hidden, cotangent, preferred_element_type=jnp.float32)
+    part_mlp = jnp.einsum(
+        "spd,spe->de", normed_two, grad_gate_up, preferred_element_type=jnp.float32
+    )
     part_out = jnp.einsum(
         "spd,spe->de", mixed_rows, grad_branch, preferred_element_type=jnp.float32
     )
-    part_mlp = jnp.einsum(
-        "spd,spe->de", normed_two, grad_gate_up, preferred_element_type=jnp.float32
-    )
-    reduced_wide = lax.psum_scatter(
-        jnp.concatenate([part_in, part_out, part_mlp, small_grads], axis=1),
-        ("batch", "seq"),
-        scatter_dimension=0,
-        tiled=True,
+    part_in = jnp.einsum("spd,spe->de", normed, grad_proj, preferred_element_type=jnp.float32)
+    small_grads = jnp.concatenate(
+        [
+            grad_taps,
+            jnp.stack([gain_grad_one, gain_grad_two], axis=-1),
+            jnp.zeros((D, SMALL - 5), jnp.float32),
+        ],
+        axis=-1,
+    )
+    last_pack = jnp.concatenate(
+        [part_in.astype(half_type), part_out.astype(half_type), small_grads.astype(half_type)],
+        axis=1,
     )
     grad_down = lax.psum_scatter(
-        jnp.einsum("spf,spd->fd", hidden, cotangent, preferred_element_type=jnp.float32),
-        ("batch", "seq"),
-        scatter_dimension=0,
-        tiled=True,
-    )
-    grad_inw = reduced_wide[:, : 3 * D]
-    grad_outw = reduced_wide[:, 3 * D : 4 * D]
-    grad_mlp = reduced_wide[:, 4 * D : 4 * D + 2 * FF]
-    grad_tapw = reduced_wide[:, 4 * D + 2 * FF : 4 * D + 2 * FF + 3]
-    grad_gains = reduced_wide[:, 4 * D + 2 * FF + 3 :]
+        part_down.astype(half_type), both, scatter_dimension=0, tiled=True
+    ).astype(jnp.float32)
+    grad_mlp = lax.psum_scatter(
+        part_mlp.astype(half_type), both, scatter_dimension=0, tiled=True
+    ).astype(jnp.float32)
+    last_sum = lax.psum_scatter(last_pack, both, scatter_dimension=0, tiled=True).astype(
+        jnp.float32
+    )
+    grad_inw = last_sum[:, : 3 * D]
+    grad_outw = last_sum[:, 3 * D : 4 * D]
+    grad_tapw = last_sum[:, 4 * D : 4 * D + 3]
+    grad_gains = last_sum[:, 4 * D + 3 : 4 * D + 5]
     rate_wide = 2.0 / D**0.5
     rate_down = 2.0 / FF**0.5
     in_new = adamw(w_in, grad_inw, first_in, second_in, rate_wide)

time: 1120 us -> 882 us (0.79)
  blocking collectives: 79.8 us -> 0 us
  local copies, waits for them, and re-layouts: 119 us -> 49 us
  waiting for transfers between devices: 715 us -> 657 us
  matrix products: 131 us -> 117 us
  other arithmetic: 47.4 us -> 33.8 us
    unnamed x7, waiting for transfers between devices: 465 us -> 78.5 us
    reduce_scatter x1 -> x2, waiting for transfers between devices: 26.2 us -> 326 us  [the longest x1 210 us: shards(): lax.psum_scatter(part_mlp.astype(half_type), both, scatter_dimension=0, t...]
    all_gather x2 -> x0, blocking collectives: 79.8 us -> none  [the longest x1 43 us: shards(): lax.all_gather(norm_gains.astype(half_type), ('batch', 'seq'), axis=0, ti...]
    concatenate x1 -> x2, local copies, waits for them, and re-layouts: 62.9 us -> 14.1 us  [the longest x1 13.3 us: shards(): jnp.concatenate([part_in.astype(half_type), part_out.astype(half_type), s...]
    all_gather x4 -> x3, waiting for transfers between devices: 224 us -> 252 us  [the longest x1 108 us: shards(): mlp_low = lax.all_gather(w_mlp.astype(half_type), both, axis=0, tiled=True)]
    unnamed x106 -> x81, local copies, waits for them, and re-layouts: 49.4 us -> 29.3 us
  transfers between devices with their start and end apart: 8 -> 8, of which waited for: 6 -> 6; matrix products, arithmetic and copies ran while one was open for 19% -> 13% of each run, Pallas kernels for 0% -> 0%
where the time goes in v1:
time: 882 us; the launch traced here: 876 us
  waiting for transfers between devices  657 us (74%)
  matrix products  117 us (13%)
  local copies, waits for them, and re-layouts  49 us (6%)
  other arithmetic  33.8 us (4%)
  between operations  15 us (2%)
    reduce_scatter x1, waiting for transfers between devices, shards(): lax.psum_scatter(part_mlp.astype(half_type), both, scatter_dimension=0, t...  210 us
    reduce_scatter x1, waiting for transfers between devices, shards(): lax.psum_scatter(part_down.astype(half_type), both, scatter_dimension=0,...  116 us
    all_gather x1, waiting for transfers between devices, shards(): mlp_low = lax.all_gather(w_mlp.astype(half_type), both, axis=0, tiled=True)  108 us
    all_gather x1, waiting for transfers between devices, shards(): first_low = lax.all_gather(first_pack, both, axis=0, tiled=True)  78.6 us
    unnamed x7, waiting for transfers between devices  78.5 us
    all_gather x1, waiting for transfers between devices, shards(): lax.all_gather(w_down.astype(half_type), both, axis=0, tiled=True)  65.4 us
    unnamed x81, local copies, waits for them, and re-layouts  29.3 us
    dot_general x1, matrix products, shards(): jnp.einsum('spd,de->spe', normed_two, mlp_low, preferred_element_type=jnp...  18.4 us
  transfers between devices with their start and end apart: 8, of which 6 were waited for; matrix products, arithmetic and copies ran while one was open for 13% of the time, Pallas kernels for 0%

profile of v1, /device:TPU:0, one launch (start us, length us, event | category | flops | bytes accessed | tf_op | source)
XLA Modules:
  0.0 876.0 jit_solution(17787135764948242943)
XLA Ops:
  14.4 78.6 %all-gather.4.cloned.1.call-done = bf16[1024,4224]{1,0:T(8,128)(2,1)} async-done(((bf16[32,4224]{1,0:T(8,128)(2,1)}), bf16[1024,4224]{1,0:T(8,128)(2,1)}) %all-gather.4.cloned.1.call-update) | async-done | bytes 8650768 | tf_op jit(solution)/shard_map/all_gather | solution.py:84
  94.5 5.7 fusion.9
  106.8 4.7 multiply_reduce_fusion.3
  111.6 108.2 %all-gather.6.cloned.1.call-done = bf16[1024,9216]{1,0:T(8,128)(2,1)} async-done(((bf16[32,9216]{1,0:T(8,128)(2,1)}), bf16[1024,9216]{1,0:T(8,128)(2,1)}) %all-gather.6.cloned.1.call-update) | async-done | bytes 18874384 | tf_op jit(solution)/shard_map/all_gather | solution.py:85
  219.8 18.4 %convolution_bitcast_fusion = f32[1,512,9216]{2,1,0:T(8,128)} fusion(bf16[1024,9216]{1,0:T(8,128)(2,1)} %all-gather.6.cloned.1.call-done, f32[1,512,1024]{2,1,0:T(8,128)} %get-tuple-element.146, f32[1024]{0:T(1024)S(1)} %get-tuple-element.100, f32[512]{0:T(512)S(1)} %get-tuple-element.144), kind=kOutput, calls=%fused_computation.1 | convolution fusion | flops 9665249280 | bytes 39852032 | tf_op jit(solution)/shard_map/spd,de->spe/dot_general | solution.py:115
  238.2 65.4 %all-gather.8.cloned.1.call-done = bf16[4608,1024]{1,0:T(8,128)(2,1)} async-done(((bf16[144,1024]{1,0:T(8,128)(2,1)}), bf16[4608,1024]{1,0:T(8,128)(2,1)}) %all-gather.8.cloned.1.call-update) | async-done | bytes 9437200 | tf_op jit(solution)/shard_map/all_gather | solution.py:86
  303.5 17.9 %fusion.14 = (bf16[512,4608]{1,0:T(8,128)(2,1)}, bf16[512,4608]{1,0:T(8,128)(2,1)}, bf16[512,4608]{1,0:T(8,128)(2,1)}) fusion(f32[1,512,9216]{2,1,0:T(8,128)} %convolution_bitcast_fusion, bf16[4608,1024]{1,0:T(8,128)(2,1)} %all-gather.8.cloned.1.call-done, bf16[1,512,1024]{2,1,0:T(8,128)(2,1)} %param.21), kind=kOutput, calls=%fused_computation.27 | convolution fusion | flops 4867227648 | bytes 43515904 | tf_op jit(solution)/shard_map/spd,fd->spf/dot_general | solution.py:122
  321.4 16.0 %fusion.28 = (bf16[1024]{0:T(1024)(128)(2,1)S(1)}, f32[512]{0:T(512)S(1)}, f32[512,1024]{1,0:T(8,128)S(1)}) fusion(f32[1,512,1024]{2,1,0:T(8,128)} %get-tuple-element.146, f32[512]{0:T(512)S(1)} %get-tuple-element.144, f32[1024]{0:T(1024)S(1)} %get-tuple-element.100, bf16[1024,9216]{1,0:T(8,128)(2,1)} %all-gather.6.cloned.1.call-done, ...), kind=kOutput, calls=%fused_computation.46 | convolution fusion | flops 9685694464 | bytes 32516096 | tf_op jit(solution)/shard_map/spe,de->spd/dot_general | solution.py:127
  338.0 3.7 fusion.34
  353.8 5.9 convolution_convert_fusion.2
  359.7 4.9 fusion.24
  366.3 13.3 %concatenate.67 = bf16[1024,4224]{1,0:T(8,128)(2,1)} concatenate(bf16[1024,3072]{1,0:T(8,128)(2,1)} %convolution_convert_fusion.2, bf16[1024,1024]{1,0:T(8,128)(2,1)S(1)} %copy-done.11, bf16[1024,1]{1,0:T(8,128)(2,1)} %stack.25, bf16[1024,1]{1,0:T(8,128)(2,1)} %stack.26, bf16[1024,1]{1,0:T(8,128)(2,1)} %stack.27, bf16[1024,1]{1,0:T(8,128)(2,1)} %stack.28, ...), dimensions={1} | concatenate | bytes 17301504 | tf_op jit(solution)/shard_map/concatenate | solution.py:172
  380.9 10.2 %convolution_convert_fusion.1 = bf16[4608,1024]{1,0:T(8,128)(2,1)} fusion(bf16[512,4608]{1,0:T(8,128)(2,1)} %get-tuple-element.136, bf16[1,512,1024]{2,1,0:T(8,128)(2,1)S(1)} %copy-done.16), kind=kOutput, calls=%fused_computation.2 | convolution fusion | flops 4836556800 | bytes 15204352 | tf_op jit(solution)/shard_map/spf,spd->fd/dot_general | solution.py:156
  392.7 17.3 %convolution_convert_fusion = bf16[1024,9216]{1,0:T(8,128)(2,1)} fusion(bf16[512,4608]{1,0:T(8,128)(2,1)} %get-tuple-element.135, bf16[512,4608]{1,0:T(8,128)(2,1)} %get-tuple-element.134, f32[1,512,1024]{2,1,0:T(8,128)S(1)} %copy-done.9, f32[1024]{0:T(1024)S(1)} %get-tuple-element.100, f32[512]{0:T(512)S(1)} %get-tuple-element.144), kind=kOutput, calls=%fused_computation | convolution fusion | flops 9693560832 | bytes 30414848 | tf_op jit(solution)/shard_map/spd,spe->de/dot_general | solution.py:157
  413.7 2.7 copy.124
  421.1 10.0 %fusion.33 = bf16[1,512,1024]{2,1,0:T(8,128)(2,1)} fusion(f32[1,512,1024]{2,1,0:T(8,128)S(1)} %copy-done.9, bf16[512,4608]{1,0:T(8,128)(2,1)} %get-tuple-element.136, bf16[4608,1024]{1,0:T(8,128)(2,1)} %all-gather.8.cloned.1.call-done), kind=kOutput, calls=%fused_computation.56 | convolution fusion | flops 4832886784 | bytes 17301504 | tf_op jit(solution)/shard_map/spf,fd->spd/dot_general | solution.py:120
  432.6 78.4 %reduce-scatter.10.cloned.1.call-done = bf16[32,4224]{1,0:T(8,128)(2,1)} async-done(((bf16[1024,4224]{1,0:T(8,128)(2,1)}), bf16[32,4224]{1,0:T(8,128)(2,1)}) %reduce-scatter.10.cloned.1.call-update) | async-done | bytes 270352
  512.7 5.3 multiply_subtract_fusion
  520.6 2.8 copy.132
  523.4 2.7 copy.133
  535.7 116.0 %reduce-scatter.8.cloned.1.call-done = bf16[144,1024]{1,0:T(8,128)(2,1)} async-done(((bf16[4608,1024]{1,0:T(8,128)(2,1)}), bf16[144,1024]{1,0:T(8,128)(2,1)}) %reduce-scatter.8.cloned.1.call-update) | async-done | bytes 294928 | tf_op jit(solution)/shard_map/reduce_scatter | solution.py:176
  651.7 3.0 multiply_subtract_fusion.2
  654.7 210.2 %reduce-scatter.6.cloned.1.call-done = bf16[32,9216]{1,0:T(8,128)(2,1)} async-done(((bf16[1024,9216]{1,0:T(8,128)(2,1)}), bf16[32,9216]{1,0:T(8,128)(2,1)}) %reduce-scatter.6.cloned.1.call-update) | async-done | bytes 589840 | tf_op jit(solution)/shard_map/reduce_scatter | solution.py:179
  864.9 3.8 multiply_subtract_fusion.1
  (136 shorter events, 55.9 us)
Async XLA Ops:
  7.2 85.8 %all-gather.4.cloned.1.call-start = ((), (), s32[]{:S(2)}) async-start(), calls=%async_computation.3 | async-start | bytes 8921088 | tf_op jit(solution)/shard_map/all_gather | solution.py:84
  11.7 208.1 %all-gather.6.cloned.1.call-start = ((), (), s32[]{:S(2)}) async-start(), calls=%async_computation.4 | async-start | bytes 19464192 | tf_op jit(solution)/shard_map/all_gather | solution.py:85
  12.7 290.9 %all-gather.8.cloned.1.call-start = ((), (), s32[]{:S(2)}) async-start(), calls=%async_computation.5 | async-start | bytes 9732096 | tf_op jit(solution)/shard_map/all_gather | solution.py:86
  13.5 497.6 %reduce-scatter.10.cloned.1.call-start = ((), (), s32[]{:S(2)}) async-start(), calls=%async_computation.8 | async-start | bytes 8921088
  100.5 3.9 collective-permute-start
  321.4 16.0 %copy-start.8 = (f32[1,512,1024]{2,1,0:T(8,128)S(1)}, f32[1,512,1024]{2,1,0:T(8,128)}, u32[]{:S(2)}) copy-start(f32[1,512,1024]{2,1,0:T(8,128)} %get-tuple-element.146) | copy-start | bytes 6291460
  321.4 16.0 %copy-start.15 = (bf16[1,512,1024]{2,1,0:T(8,128)(2,1)S(1)}, bf16[1,512,1024]{2,1,0:T(8,128)(2,1)}, u32[]{:S(2)}) copy-start(bf16[1,512,1024]{2,1,0:T(8,128)(2,1)} %param.21) | copy-start | bytes 3145732
  338.0 7.8 copy-start.1
  344.3 4.5 collective-permute-start.1
  349.0 10.7 %slice-start.2 = ((s8[8650752]{0:T(1024)(128)(4,1)}), s8[4194304]{0:T(1024)(128)(4,1)S(1)}, s32[]{:S(2)}) async-start(s8[8650752]{0:T(1024)(128)(4,1)} %bitcast.97), calls=%async_computation.11 | async-start | bytes 8388608
  349.0 10.7 %slice-start.3 = ((s8[8650752]{0:T(1024)(128)(4,1)}), s8[4194304]{0:T(1024)(128)(4,1)S(1)}, s32[]{:S(2)}) async-start(s8[8650752]{0:T(1024)(128)(4,1)} %bitcast.97), calls=%async_computation.12 | async-start | bytes 8388608
  379.7 272.0 %reduce-scatter.8.cloned.1.call-start = ((), (), s32[]{:S(2)}) async-start(), calls=%async_computation.7 | async-start | bytes 9732096 | tf_op jit(solution)/shard_map/reduce_scatter | solution.py:176
  391.1 473.8 %reduce-scatter.6.cloned.1.call-start = ((), (), s32[]{:S(2)}) async-start(), calls=%async_computation.6 | async-start | bytes 19464192 | tf_op jit(solution)/shard_map/reduce_scatter | solution.py:179
  421.1 10.0 %copy-start.2 = (f32[1,512,1024]{2,1,0:T(8,128)S(1)}, f32[1,512,1024]{2,1,0:T(8,128)}, u32[]{:S(2)}) copy-start(f32[1,512,1024]{2,1,0:T(8,128)} %copy-done.1) | copy-start | bytes 6291460
  421.1 10.0 %copy-start.10 = (f32[512,1024]{1,0:T(8,128)S(1)}, f32[512,1024]{1,0:T(8,128)}, u32[]{:S(2)}) copy-start(f32[512,1024]{1,0:T(8,128)} %get-tuple-element.148) | copy-start | bytes 6291460
  421.1 10.0 %copy-start.22 = (f32[512]{0:T(512)S(1)}, f32[512]{0:T(512)}, u32[]{:S(2)}) copy-start(f32[512]{0:T(512)} %get-tuple-element.141) | copy-start | bytes 6148
  526.1 8.4 copy-start.26
  526.1 8.4 copy-start.27
  526.1 8.4 copy-start.28
  526.1 8.9 %copy-start.23 = (f32[32,3]{0,1:T(4,128)S(1)}, f32[32,3]{0,1:T(4,128)}, u32[]{:S(2)}) copy-start(f32[32,3]{0,1:T(4,128)} %param.25) | copy-start | bytes 1156
  526.1 8.9 %copy-start.24 = (f32[32,3]{0,1:T(4,128)S(1)}, f32[32,3]{0,1:T(4,128)}, u32[]{:S(2)}) copy-start(f32[32,3]{0,1:T(4,128)} %param.27) | copy-start | bytes 1156
  526.2 8.9 %copy-start.25 = (f32[32,3]{0,1:T(4,128)S(1)}, f32[32,3]{0,1:T(4,128)}, u32[]{:S(2)}) copy-start(f32[32,3]{0,1:T(4,128)} %param.26) | copy-start | bytes 1156
  532.5 332.4 %copy-start.5 = (f32[32,9216]{1,0:T(8,128)S(1)}, f32[32,9216]{1,0:T(8,128)}, u32[]{:S(2)}) copy-start(f32[32,9216]{1,0:T(8,128)} %param.31) | copy-start | bytes 3538948
  535.7 329.2 %copy-start.14 = (f32[32,9216]{1,0:T(8,128)S(1)}, f32[32,9216]{1,0:T(8,128)}, u32[]{:S(2)}) copy-start(f32[32,9216]{1,0:T(8,128)} %param.33) | copy-start | bytes 3538948
  (18 other events, 80.5 us)
Sparse Core Ops, SparseCore 0:
  11.8 81.1 all-gather.3
  96.5 123.2 all-gather.5
  223.3 80.2 all-gather.7
  379.8 131.2 reduce-scatter.9
  516.8 134.8 reduce-scatter.7
  659.1 205.7 reduce-scatter.5

commit v2 on v1

--- a/solution.py
+++ b/solution.py
@@ -20,6 +20,27 @@
     devices = range(lax.axis_size(axis))
     route = [(i - distance, i) for i in devices if i - distance in devices]
     return lax.ppermute(block, axis, route)
+
+
+def paired():
+    return lax.axis_size("seq") == 2 and D % (32 * lax.axis_size("batch")) == 0
+
+
+def core_sum(part):
+    if not paired():
+        return part
+    me = lax.axis_index("seq")
+    blocks = part.reshape(lax.axis_size("batch"), 2, -1, part.shape[1])
+    theirs = lax.dynamic_index_in_dim(blocks, 1 - me, axis=1, keepdims=False)
+    mine = lax.dynamic_index_in_dim(blocks, me, axis=1, keepdims=False)
+    arrived = lax.ppermute(theirs, "seq", [(0, 1), (1, 0)])
+    total = mine.astype(jnp.float32) + arrived.astype(jnp.float32)
+    return total.astype(part.dtype).reshape(-1, part.shape[1])
+
+
+def spread_sum(half):
+    axes = "batch" if paired() else ("batch", "seq")
+    return lax.psum_scatter(half, axes, scatter_dimension=0, tiled=True)
 
 
 def rms_scale(values):
@@ -71,8 +92,9 @@
     rows = w_in.shape[0]
     both = ("batch", "seq")
     spare = jnp.zeros((rows, SMALL - 5), half_type)
-    first_pack = jnp.concatenate(
-        [
+    wide_pack = jnp.concatenate(
+        [
+            w_mlp.astype(half_type),
             w_in.astype(half_type),
             w_out.astype(half_type),
             conv_taps.astype(half_type),
@@ -81,13 +103,13 @@
         ],
         axis=1,
     )
-    first_low = lax.all_gather(first_pack, both, axis=0, tiled=True)
-    mlp_low = lax.all_gather(w_mlp.astype(half_type), both, axis=0, tiled=True)
+    wide_low = lax.all_gather(wide_pack, both, axis=0, tiled=True)
     down_low = lax.all_gather(w_down.astype(half_type), both, axis=0, tiled=True)
-    in_low = first_low[:, : 3 * D]
-    out_low = first_low[:, 3 * D : 4 * D]
-    conv_low = first_low[:, 4 * D : 4 * D + 3]
-    gain_low = first_low[:, 4 * D + 3 : 4 * D + 5]
+    mlp_low = wide_low[:, : 2 * FF]
+    in_low = wide_low[:, 2 * FF : 2 * FF + 3 * D]
+    out_low = wide_low[:, 2 * FF + 3 * D : 2 * FF + 4 * D]
+    conv_low = wide_low[:, 2 * FF + 4 * D : 2 * FF + 4 * D + 3]
+    gain_low = wide_low[:, 2 * FF + 4 * D + 3 : 2 * FF + 4 * D + 5]
     tap_values = conv_low.astype(jnp.float32)
     gain_one = gain_low[:, 0].astype(jnp.float32)
     gain_two = gain_low[:, 1].astype(jnp.float32)
@@ -127,6 +149,10 @@
     grad_normed_two = jnp.einsum(
         "spe,de->spd", grad_gate_up, mlp_low, preferred_element_type=jnp.float32
     )
+    part_down = jnp.einsum("spf,spd->fd", hidden, cotangent, preferred_element_type=jnp.float32)
+    down_half = core_sum(part_down.astype(half_type))
+    down_half, grad_normed_two = lax.optimization_barrier((down_half, grad_normed_two))
+    down_sum = spread_sum(down_half)
     grad_middle, gain_grad_two = norm_back(middle, scale_two, gain_two, grad_normed_two)
     grad_middle = cotangent.astype(jnp.float32) + grad_middle
     grad_branch = grad_middle.astype(half_type)
@@ -153,7 +179,6 @@
     grad_normed = jnp.einsum("spe,de->spd", grad_proj, in_low, preferred_element_type=jnp.float32)
     grad_inputs, gain_grad_one = norm_back(inputs, scale_one, gain_one, grad_normed)
     grad_tokens = (grad_middle + grad_inputs).astype(half_type)
-    part_down = jnp.einsum("spf,spd->fd", hidden, cotangent, preferred_element_type=jnp.float32)
     part_mlp = jnp.einsum(
         "spd,spe->de", normed_two, grad_gate_up, preferred_element_type=jnp.float32
     )
@@ -169,19 +194,18 @@
         ],
         axis=-1,
     )
-    last_pack = jnp.concatenate(
-        [part_in.astype(half_type), part_out.astype(half_type), small_grads.astype(half_type)],
+    wide_half = jnp.concatenate(
+        [
+            core_sum(part.astype(half_type))
+            for part in (part_mlp, part_in, part_out, small_grads)
+        ],
         axis=1,
     )
-    grad_down = lax.psum_scatter(
-        part_down.astype(half_type), both, scatter_dimension=0, tiled=True
-    ).astype(jnp.float32)
-    grad_mlp = lax.psum_scatter(
-        part_mlp.astype(half_type), both, scatter_dimension=0, tiled=True
-    ).astype(jnp.float32)
-    last_sum = lax.psum_scatter(last_pack, both, scatter_dimension=0, tiled=True).astype(
-        jnp.float32
-    )
+    wide_half, down_sum = lax.optimization_barrier((wide_half, down_sum))
+    grad_down = down_sum.astype(jnp.float32)
+    wide_sum = spread_sum(wide_half).astype(jnp.float32)
+    grad_mlp = wide_sum[:, : 2 * FF]
+    last_sum = wide_sum[:, 2 * FF :]
     grad_inw = last_sum[:, : 3 * D]
     grad_outw = last_sum[:, 3 * D : 4 * D]
     grad_tapw = last_sum[:, 4 * D : 4 * D + 3]

time: 882 us -> 776 us (0.88)
  waiting for transfers between devices: 657 us -> 477 us
  other arithmetic: 33.8 us -> 84.9 us
  local copies, waits for them, and re-layouts: 49 us -> 77.1 us
    reduce_scatter x2 -> x1, waiting for transfers between devices: 326 us -> 71.3 us  [spread_sum(): return lax.psum_scatter(half, axes, scatter_dimension=0, tiled=True)]
    unnamed x7 -> x5, waiting for transfers between devices: 78.5 us -> 188 us
    unnamed x81 -> x103, local copies, waits for them, and re-layouts: 29.3 us -> 55.5 us
    convert_element_type x2 -> x7, other arithmetic: 1.02 us -> 24.2 us  [the longest x5 22.3 us: core_sum(): return total.astype(part.dtype).reshape(-1, part.shape[1])]
    all_gather x2 -> x1, waiting for transfers between devices: 187 us -> 167 us  [shards(): wide_low = lax.all_gather(wide_pack, both, axis=0, tiled=True)]
    all_gather x1, waiting for transfers between devices: 65.4 us -> 47.3 us  [shards(): lax.all_gather(w_down.astype(half_type), both, axis=0, tiled=True)]
    concatenate x0 -> x1, other arithmetic: none -> 14.7 us  [shards(): jnp.concatenate([core_sum(part.astype(half_type)) for part in (part_mlp,...]
    squeeze x0 -> x5, local copies, waits for them, and re-layouts: none -> 13.9 us  [core_sum(): theirs = lax.dynamic_index_in_dim(blocks, 1 - me, axis=1, keepdims=False)]
  transfers between devices with their start and end apart: 8 -> 11, of which waited for: 6 -> 6; matrix products, arithmetic and copies ran while one was open for 13% -> 24% of each run, Pallas kernels for 0% -> 0%
where the time goes in v2:
time: 776 us; the launch traced here: 772 us
  waiting for transfers between devices  477 us (61%)
  matrix products  114 us (15%)
  other arithmetic  84.9 us (11%)
  local copies, waits for them, and re-layouts  77.1 us (10%)
  between operations  14.6 us (2%)
    unnamed x5, waiting for transfers between devices  188 us
    all_gather x1, waiting for transfers between devices, shards(): wide_low = lax.all_gather(wide_pack, both, axis=0, tiled=True)  167 us
    reduce_scatter x1, waiting for transfers between devices, spread_sum(): return lax.psum_scatter(half, axes, scatter_dimension=0, tiled=True)  71.3 us
    unnamed x103, local copies, waits for them, and re-layouts  55.5 us
    all_gather x1, waiting for transfers between devices, shards(): lax.all_gather(w_down.astype(half_type), both, axis=0, tiled=True)  47.3 us
    convert_element_type x5, other arithmetic, core_sum(): return total.astype(part.dtype).reshape(-1, part.shape[1])  22.3 us
    sub x6, other arithmetic, adamw(): weight - learn_rate * (first_hat / (jnp.sqrt(second_hat) + ADAM_EPS) + DE...  21.8 us
    dot_general x1, matrix products, shards(): jnp.einsum('spd,fd->spf', cotangent, down_low, preferred_element_type=jnp...  19.7 us
  transfers between devices with their start and end apart: 11, of which 6 were waited for; matrix products, arithmetic and copies ran while one was open for 24% of the time, Pallas kernels for 0%

profile of v2, /device:TPU:0, one launch (start us, length us, event | category | flops | bytes accessed | tf_op | source)
XLA Modules:
  0.0 772.1 jit_solution(13655391521617080078)
XLA Ops:
  15.1 167.0 %all-gather.3.cloned.1.call-done = bf16[1024,13440]{1,0:T(8,128)(2,1)} async-done(((bf16[32,13440]{1,0:T(8,128)(2,1)}), bf16[1024,13440]{1,0:T(8,128)(2,1)}) %all-gather.3.cloned.1.call-update) | async-done | bytes 27525136 | tf_op jit(solution)/shard_map/all_gather | solution.py:106
  183.7 5.7 fusion.18
  200.9 17.6 %fusion.5 = f32[1,512,9216]{2,1,0:T(8,128)} fusion(bf16[1024,13440]{1,0:T(8,128)(2,1)} %all-gather.3.cloned.1.call-done, f32[1,512,1024]{2,1,0:T(8,128)S(1)} %get-tuple-element.154, f32[1024]{0:T(1024)S(1)} %get-tuple-element.108, f32[512]{0:T(512)S(1)} %get-tuple-element.152), kind=kOutput, calls=%fused_computation.7 | convolution fusion | flops 9665249280 | bytes 39852032 | tf_op jit(solution)/shard_map/spd,de->spe/dot_general | solution.py:137
  218.5 47.3 %all-gather.5.cloned.1.call-done = bf16[4608,1024]{1,0:T(8,128)(2,1)} async-done(((bf16[144,1024]{1,0:T(8,128)(2,1)}), bf16[4608,1024]{1,0:T(8,128)(2,1)}) %all-gather.5.cloned.1.call-update) | async-done | bytes 9437200 | tf_op jit(solution)/shard_map/all_gather | solution.py:107
  265.8 19.7 %fusion.24 = (bf16[512,4608]{1,0:T(8,128)(2,1)}, bf16[512,4608]{1,0:T(8,128)(2,1)}, bf16[512,4608]{1,0:T(8,128)(2,1)}) fusion(f32[1,512,9216]{2,1,0:T(8,128)} %fusion.5, bf16[4608,1024]{1,0:T(8,128)(2,1)} %all-gather.5.cloned.1.call-done, bf16[1,512,1024]{2,1,0:T(8,128)(2,1)S(1)} %copy-done.23), kind=kOutput, calls=%fused_computation.43 | convolution fusion | flops 4867227648 | bytes 43515904 | tf_op jit(solution)/shard_map/spd,fd->spf/dot_general | solution.py:144
  285.5 7.7 convolution_convert_fusion.1
  296.0 4.1 copy-done.2
  300.9 14.6 %convolution_convert_fusion = bf16[1024,9216]{1,0:T(8,128)(2,1)} fusion(bf16[512,4608]{1,0:T(8,128)(2,1)} %get-tuple-element.143, bf16[512,4608]{1,0:T(8,128)(2,1)S(1)} %copy-done.41, f32[1,512,1024]{2,1,0:T(8,128)S(1)} %copy-done.6, f32[1024]{0:T(1024)S(1)} %get-tuple-element.108, f32[512]{0:T(512)S(1)} %get-tuple-element.152), kind=kOutput, calls=%fused_computation.2 | convolution fusion | flops 9693560832 | bytes 30414848 | tf_op jit(solution)/shard_map/spd,spe->de/dot_general | solution.py:182
  315.5 8.1 %dynamic-slice_bitcast_fusion = bf16[16,32,9216]{2,1,0:T(8,128)(2,1)} fusion(bf16[16,2,32,9216]{3,2,1,0:T(8,128)(2,1)} %bitcast.123, s32[]{:T(128)S(6)} %select_n.20), kind=kLoop, calls=%fused_computation.18 | loop fusion | bytes 18874372 | tf_op jit(solution)/shard_map/jit(dynamic_index_in_dim)/squeeze | solution.py:34
  323.8 15.7 %fusion.45 = f32[1,512,1024]{2,1,0:T(8,128)} fusion(bf16[1024,13440]{1,0:T(8,128)(2,1)} %all-gather.3.cloned.1.call-done, bf16[512,4608]{1,0:T(8,128)(2,1)} %get-tuple-element.143, bf16[512,4608]{1,0:T(8,128)(2,1)} %get-tuple-element.142), kind=kOutput, calls=%fused_computation.87 | convolution fusion | flops 9682550784 | bytes 30408704 | tf_op jit(solution)/shard_map/spe,de->spd/dot_general | solution.py:149
  339.6 8.5 %fusion.8 = bf16[16,144,1024]{2,1,0:T(8,128)(2,1)} fusion(bf16[16,144,1024]{2,1,0:T(8,128)(2,1)} %collective-permute-done.1, bf16[16,2,144,1024]{3,2,1,0:T(8,128)(2,1)} %bitcast.127, s32[]{:T(128)S(6)} %select_n.19), kind=kLoop, calls=%fused_computation.12 | loop fusion | flops 9437184 | bytes 14155780 | tf_op jit(solution)/shard_map/convert_element_type | solution.py:38
  368.1 4.2 convolution_convert_fusion.2
  385.1 8.9 %fusion.34 = (bf16[1024]{0:T(1024)(128)(2,1)S(1)}, f32[512]{0:T(512)S(1)}, f32[512,1024]{1,0:T(8,128)}) fusion(bf16[1,512,1024]{2,1,0:T(8,128)(2,1)S(1)} %copy-done.16, f32[512]{0:T(512)S(1)} %get-tuple-element.150, f32[1024]{0:T(1024)S(1)} %get-tuple-element.109, bf16[1024,13440]{1,0:T(8,128)(2,1)} %all-gather.3.cloned.1.call-done, ...), kind=kOutput, calls=%fused_computation.56 | convolution fusion | flops 3234331136 | bytes 12593152 | tf_op jit(solution)/shard_map/spe,de->spd/dot_general | solution.py:179
  399.5 4.1 fusion.13
  403.6 7.7 %fusion = bf16[16,32,9216]{2,1,0:T(8,128)(2,1)S(1)} fusion(bf16[16,32,9216]{2,1,0:T(8,128)(2,1)} %collective-permute-done.3, bf16[16,2,32,9216]{3,2,1,0:T(8,128)(2,1)} %bitcast.124, s32[]{:T(128)S(6)} %select_n.19), kind=kLoop, calls=%fused_computation.1 | loop fusion | flops 18874368 | bytes 28311556 | tf_op jit(solution)/shard_map/convert_element_type | solution.py:38
  411.4 14.7 %pad_maximum_fusion = bf16[512,13440]{1,0:T(8,128)(2,1)} fusion(bf16[512,128]{1,0:T(8,128)(2,1)S(1)} %bitcast.133, bf16[512,1024]{1,0:T(8,128)(2,1)S(1)} %bitcast.130, bf16[512,3072]{1,0:T(8,128)(2,1)S(1)} %bitcast.125, bf16[512,9216]{1,0:T(8,128)(2,1)S(1)} %bitcast.121), kind=kLoop, calls=%fused_computation.8 | loop fusion | flops 55050240 | bytes 27525120 | tf_op jit(solution)/shard_map/concatenate | solution.py:197
  426.1 71.3 %reduce-scatter.5.cloned.1.call-done = bf16[144,1024]{1,0:T(8,128)(2,1)} async-done(((bf16[2304,1024]{1,0:T(8,128)(2,1)}), bf16[144,1024]{1,0:T(8,128)(2,1)}) %reduce-scatter.5.cloned.1.call-update) | async-done | bytes 294928 | tf_op jit(solution)/shard_map/reduce_scatter | solution.py:43
  514.5 3.9 copy.153
  518.4 10.3 %fusion.40 = bf16[1,512,1024]{2,1,0:T(8,128)(2,1)} fusion(f32[1,512,1024]{2,1,0:T(8,128)} %copy-done.5, bf16[512,4608]{1,0:T(8,128)(2,1)} %get-tuple-element.144, bf16[4608,1024]{1,0:T(8,128)(2,1)} %all-gather.5.cloned.1.call-done), kind=kOutput, calls=%fused_computation.68 | convolution fusion | flops 4832886784 | bytes 17301504 | tf_op jit(solution)/shard_map/spf,fd->spd/dot_general | solution.py:142
  532.1 188.1 %reduce-scatter.7.cloned.1.call-done = bf16[32,13440]{1,0:T(8,128)(2,1)} async-done(((bf16[512,13440]{1,0:T(8,128)(2,1)}), bf16[32,13440]{1,0:T(8,128)(2,1)}) %reduce-scatter.7.cloned.1.call-update) | async-done | bytes 860176
  738.2 12.9 %multiply_subtract_fusion = (f32[32,9216]{0,1:T(8,128)}, f32[32,9216]{0,1:T(8,128)}, f32[32,9216]{0,1:T(8,128)}) fusion(f32[32,9216]{0,1:T(8,128)} %copy.156, f32[32,13440]{0,1:T(8,128)} %copy-done, f32[32,9216]{0,1:T(8,128)} %copy.154, f32[32,9216]{0,1:T(8,128)} %copy.153), kind=kLoop, calls=%fused_computation.34 | loop fusion | flops 4423680 | bytes 8257536 | tf_op jit(solution)/shard_map/sub | solution.py:63
  751.2 3.8 copy.163
  755.0 3.8 copy.164
  758.9 3.9 copy.165
  (177 shorter events, 103.9 us)
Async XLA Ops:
  7.2 6.2 copy-start.18
  7.2 7.0 copy-start.15
  7.2 174.9 %all-gather.3.cloned.1.call-start = ((), (), s32[]{:S(2)}) async-start(), calls=%async_computation.2 | async-start | bytes 28385280 | tf_op jit(solution)/shard_map/all_gather | solution.py:106
  13.3 252.5 %all-gather.5.cloned.1.call-start = ((), (), s32[]{:S(2)}) async-start(), calls=%async_computation.3 | async-start | bytes 9732096 | tf_op jit(solution)/shard_map/all_gather | solution.py:107
  14.1 483.3 %reduce-scatter.5.cloned.1.call-start = ((), (), s32[]{:S(2)}) async-start(), calls=%async_computation.4 | async-start | bytes 5013504 | tf_op jit(solution)/shard_map/reduce_scatter | solution.py:43
  189.7 4.1 collective-permute-start
  200.9 64.9 %copy-start.23 = (bf16[1,512,1024]{2,1,0:T(8,128)(2,1)S(1)}, bf16[1,512,1024]{2,1,0:T(8,128)(2,1)}, u32[]{:S(2)}) copy-start(bf16[1,512,1024]{2,1,0:T(8,128)(2,1)} %param.21) | copy-start | bytes 3145732
  293.2 6.9 copy-start.2
  293.2 7.2 copy-start.6
  293.2 7.7 %copy-start.41 = (bf16[512,4608]{1,0:T(8,128)(2,1)S(1)}, bf16[512,4608]{1,0:T(8,128)(2,1)}, u32[]{:S(2)}) copy-start(bf16[512,4608]{1,0:T(8,128)(2,1)} %get-tuple-element.142) | copy-start | bytes 14155780
  300.1 39.5 %collective-permute-start.1 = (bf16[16,144,1024]{2,1,0:T(8,128)(2,1)}, bf16[16,144,1024]{2,1,0:T(8,128)(2,1)}, u32[]{:S(2)}, u32[]{:S(2)}) collective-permute-start(bf16[16,144,1024]{2,1,0:T(8,128)(2,1)} %dynamic-slice_bitcast_fusion.1), channel_id=1, source_target_pairs={{0,1},{1,0},{2,3},{3,2},{4,5},{5,4},{6,7},{7,6},{8,9},{9,8},{10,11... | collective-permute-start | bytes 14155784 | tf_op jit(solution)/shard_map/ppermute | solution.py:36
  323.6 80.1 %collective-permute-start.3 = (bf16[16,32,9216]{2,1,0:T(8,128)(2,1)}, bf16[16,32,9216]{2,1,0:T(8,128)(2,1)}, u32[]{:S(2)}, u32[]{:S(2)}) collective-permute-start(bf16[16,32,9216]{2,1,0:T(8,128)(2,1)} %dynamic-slice_bitcast_fusion), channel_id=1, source_target_pairs={{0,1},{1,0},{2,3},{3,2},{4,5},{5,4},{6,7},{7,6},{8,9},{9,8},{10,11... | collective-permute-start | bytes 28311560 | tf_op jit(solution)/shard_map/ppermute | solution.py:36
  359.3 3.0 collective-permute-start.2
  360.6 359.6 %reduce-scatter.7.cloned.1.call-start = ((), (), s32[]{:S(2)}) async-start(), calls=%async_computation.5 | async-start | bytes 14622720
  365.5 6.8 copy-start.27
  376.2 23.4 %collective-permute-start.4 = (bf16[16,32,3072]{2,1,0:T(8,128)(2,1)}, bf16[16,32,3072]{2,1,0:T(8,128)(2,1)}, u32[]{:S(2)}, u32[]{:S(2)}) collective-permute-start(bf16[16,32,3072]{2,1,0:T(8,128)(2,1)} %dynamic-slice_bitcast_fusion.2), channel_id=1, source_target_pairs={{0,1},{1,0},{2,3},{3,2},{4,5},{5,4},{6,7},{7,6},{8,9},{9,8},{10,11... | collective-permute-start | bytes 9437192 | tf_op jit(solution)/shard_map/ppermute | solution.py:36
  381.6 16.0 %collective-permute-start.5 = (bf16[16,32,1024]{2,1,0:T(8,128)(2,1)}, bf16[16,32,1024]{2,1,0:T(8,128)(2,1)}, u32[]{:S(2)}, u32[]{:S(2)}) collective-permute-start(bf16[16,32,1024]{2,1,0:T(8,128)(2,1)} %dynamic-slice_bitcast_fusion.3), channel_id=1, source_target_pairs={{0,1},{1,0},{2,3},{3,2},{4,5},{5,4},{6,7},{7,6},{8,9},{9,8},{10,11... | collective-permute-start | bytes 3145736 | tf_op jit(solution)/shard_map/ppermute | solution.py:36
  396.1 1.4 collective-permute-start.6
  426.1 74.1 %copy-start.30 = (f32[32,1024]{1,0:T(8,128)S(1)}, f32[32,1024]{1,0:T(8,128)}, u32[]{:S(2)}) copy-start(f32[32,1024]{1,0:T(8,128)} %param.28) | copy-start | bytes 393220
  504.1 6.4 copy-start.33
  504.1 7.4 copy-start.22
  518.4 10.3 %copy-start.17 = (bf16[1,512,1024]{2,1,0:T(8,128)(2,1)S(1)}, bf16[1,512,1024]{2,1,0:T(8,128)(2,1)}, u32[]{:S(2)}) copy-start(bf16[1,512,1024]{2,1,0:T(8,128)(2,1)} %param.20) | copy-start | bytes 3145732
  518.4 10.3 %copy-start.20 = (f32[512,1024]{1,0:T(8,128)S(1)}, f32[512,1024]{1,0:T(8,128)}, u32[]{:S(2)}) copy-start(f32[512,1024]{1,0:T(8,128)} %get-tuple-element.155) | copy-start | bytes 6291460
  518.4 10.3 %copy-start.34 = (f32[512]{0:T(512)S(1)}, f32[512]{0:T(512)}, u32[]{:S(2)}) copy-start(f32[512]{0:T(512)} %get-tuple-element.149) | copy-start | bytes 6148
  (29 other events, 94.5 us)
Sparse Core Ops, SparseCore 0:
  13.4 168.6 all-gather.2
  185.6 80.2 all-gather.4
  360.7 136.6 reduce-scatter.4
  504.1 216.0 reduce-scatter.6
